TPU v7x, 512 devices: a whole 4x8x8 slice. The times are simulated.
512 devices in a mesh: section: 16 (over y, z_hi), dp: 16 (over z_lo, x), cores: 2 (over core).
Axes of the slice: x: 4, y: 8, z: 8 (z_hi: 2, z_lo: 4; z = z_hi * 4 + z_lo), core: 2. Of those that a mesh axis runs over, the one named last changes fastest.
Arguments:
- arrivals: bfloat16 [2, 1536, 2048], P(None, 'dp'), may hold values from -6 to 6
- in_flight: bfloat16 [16, 1536, 2048], P('section', 'dp'), may hold values from -6 to 6
- cotangent: bfloat16 [2, 1536, 2048], P(None, 'dp'), may hold values from -6 to 6
- grad_flight: bfloat16 [16, 1536, 2048], P('section', 'dp'), may hold values from -6 to 6
- stashed: bfloat16 [16, 2, 1536, 2048], P('section', None, 'dp'), may hold values from -6 to 6
- in_weight: bfloat16 [16, 2048, 4096], P('section', 'dp', 'cores'), may hold values from -0.125 to 0.125
- out_weight: bfloat16 [16, 1024, 2048], P('section', 'cores', 'dp'), may hold values from -0.1875 to 0.1875
- forward_blocks: int32 [16, 17], P('dp'), may hold values from 1 to 4, 42 in all within a row
- backward_blocks: int32 [16, 17], P('dp'), may hold values from 1 to 4, 42 in all within a row
- forward_marks: int32 [16, 17, 4, 4], P('dp'), may hold values 0 or 1
- backward_marks: int32 [16, 17, 4, 4], P('dp'), may hold values 0 or 1
Outputs:
- activations: bfloat16 [16, 2, 1536, 2048], P('section', None, ('dp', 'cores'))
- input_grads: bfloat16 [16, 2, 1536, 2048], P('section', None, ('dp', 'cores'))
- weight_grads: float32 [16, 1024, 2048], P('section', 'cores', 'dp')
Inputs may be any that keep to these rules, and one draw needn't show every extreme that they name: `forward_blocks`: in each replica's row the 17 lengths add up to 42 blocks and the longest is 4. `backward_blocks`: in each replica's row the 17 lengths add up to 42 blocks and the longest is 4.
All inputs are finite; a program needn't handle non-finite values. No bound on the sum of `forward_marks` or of `backward_marks` on one device may be relied on, other than what follows from the above.
Results may differ from a plain program's by a relative error of at most 0.03.
Values may be sent and summed in bfloat16 or wider, within the bound.
A program may use at most 64 MiB of HBM per device.

v0:
```python
import jax
import jax.numpy as jnp
from jax import lax
from jax.sharding import PartitionSpec as P

HEAD_DIM = 128
BLOCK = 24
BLOCKS = 4
EPSILON = 1e-06


def from_behind(x, axis, by):
    peers = lax.axis_size(axis)
    pairs = [(i, i + by) for i in range(peers) if 0 <= i + by < peers]
    return lax.ppermute(x, axis, pairs)


def block_keep(live_blocks, block_marks):
    length = BLOCKS * BLOCK
    places = jnp.arange(length, dtype=jnp.int32)
    owners = places // BLOCK
    onehot = (owners[:, None] == jnp.arange(BLOCKS, dtype=jnp.int32)[None, :]).astype(jnp.float32)
    spread = jnp.einsum("ia,rab,jb->rij", onehot, block_marks.astype(jnp.float32), onehot)
    allowed = (owners[:, None] == owners[None, :])[None] | (spread > 0.5)
    causal = (places[:, None] >= places[None, :])[None]
    tokens_live = live_blocks * BLOCK
    living = places[None, :] < tokens_live[:, None]
    keeping = causal & allowed & living[:, :, None] & living[:, None, :]
    return (keeping.astype(jnp.float32), 1.0 / tokens_live.astype(jnp.float32))


def choose_history(block_table, mark_table, history):
    histories = block_table.shape[1]
    matches = jnp.arange(histories, dtype=jnp.int32) == history
    blocks = jnp.sum(jnp.where(matches, block_table[0], 0))
    marked = jnp.sum(jnp.where(matches[:, None, None], mark_table[0], 0), axis=0)
    return block_keep(blocks[None], marked[None])


def norm_rows(values_f):
    return lax.rsqrt(jnp.mean(values_f * values_f, axis=-1, keepdims=True) + EPSILON)


def heads_forward(pre_act, keeping, inverse_count):
    scaling = HEAD_DIM ** (-0.5)
    active = jax.nn.silu(pre_act)
    gate_rows = active[:, :, :, 0]
    value_rows = active[:, :, :, 1].astype(jnp.bfloat16)
    query_rows = active[:, :, :, 2].astype(jnp.bfloat16)
    key_rows = active[:, :, :, 3].astype(jnp.bfloat16)
    scores = (
        jnp.einsum("rigd,rjgd->rgij", query_rows, key_rows, preferred_element_type=jnp.float32)
        * scaling
    )
    weights = keeping[:, None] * inverse_count[:, None, None, None]
    attention = (jax.nn.silu(scores) * weights).astype(jnp.bfloat16)
    mixed = jnp.einsum("rgij,rjgd->rigd", attention, value_rows, preferred_element_type=jnp.float32)
    root_scale = lax.rsqrt(jnp.mean(mixed * mixed, axis=-1, keepdims=True) + EPSILON)
    normed = mixed * root_scale
    gated = (normed * gate_rows).astype(jnp.bfloat16)
    return (
        gated,
        (
            gate_rows,
            value_rows,
            query_rows,
            key_rows,
            scores,
            weights,
            attention,
            root_scale,
            normed,
        ),
    )


def heads_backward(pre_act, saved, upstream):
    gate_rows, value_rows, query_rows, key_rows, scores, weights, attention, root_scale, normed = (
        saved
    )
    scaling = HEAD_DIM ** (-0.5)
    grad_gated = upstream.astype(jnp.float32)
    grad_normed = grad_gated * gate_rows
    grad_gate = grad_gated * normed
    grad_mixed = root_scale * (
        grad_normed - normed * jnp.mean(grad_normed * normed, axis=-1, keepdims=True)
    )
    mixed_low = grad_mixed.astype(jnp.bfloat16)
    grad_attention = jnp.einsum(
        "rigd,rjgd->rgij", mixed_low, value_rows, preferred_element_type=jnp.float32
    )
    grad_value = jnp.einsum(
        "rgij,rigd->rjgd", attention, mixed_low, preferred_element_type=jnp.float32
    )
    sigmoid_s = jax.nn.sigmoid(scores)
    grad_scores = (
        grad_attention * weights * sigmoid_s * (1.0 + scores * (1.0 - sigmoid_s)) * scaling
    ).astype(jnp.bfloat16)
    grad_query = jnp.einsum(
        "rgij,rjgd->rigd", grad_scores, key_rows, preferred_element_type=jnp.float32
    )
    grad_key = jnp.einsum(
        "rgij,rigd->rjgd", grad_scores, query_rows, preferred_element_type=jnp.float32
    )
    grad_active = jnp.stack([grad_gate, grad_value, grad_query, grad_key], axis=3)
    sigmoid_u = jax.nn.sigmoid(pre_act)
    return (grad_active * sigmoid_u * (1.0 + pre_act * (1.0 - sigmoid_u))).astype(jnp.bfloat16)


def per_device(
    arrivals,
    in_flight,
    cotangent,
    grad_flight,
    stashed,
    in_weight,
    out_weight,
    forward_blocks,
    backward_blocks,
    forward_marks,
    backward_marks,
):
    section_no = lax.axis_index("section")
    sections = lax.axis_size("section")
    core_no = lax.axis_index("cores")
    ticks = arrivals.shape[0]
    length = arrivals.shape[1]
    share = length // lax.axis_size("cores")
    row_start = core_no * share
    out_full = lax.all_gather(out_weight[0], "dp", axis=1, tiled=True)
    slab_rows = out_full.shape[0]
    groups = slab_rows // HEAD_DIM
    columns = in_weight.shape[2]
    in_full = None
    in_full = lax.all_gather(in_weight[0], "dp", axis=0, tiled=True)
    received = in_flight[0]
    returned = grad_flight[0]
    ahead_out = []
    back_out = []
    gated_list = []
    upstream_list = []
    for tick_no in range(ticks):
        if tick_no == 0:
            prior = in_flight[0]
            later = grad_flight[0]
        else:
            prior = received
            later = returned
        inputs = jnp.where(section_no == 0, arrivals[tick_no], prior)
        upstream = jnp.where(section_no == sections - 1, cotangent[tick_no], later)
        keep_ahead, count_ahead = choose_history(
            forward_blocks, forward_marks, tick_no - section_no + sections - 1
        )
        keep_back, count_back = choose_history(
            backward_blocks, backward_marks, tick_no + section_no
        )
        floats = inputs.astype(jnp.float32)
        saved_floats = stashed[0, tick_no].astype(jnp.float32)
        root_saved = norm_rows(saved_floats)
        scaled_saved = saved_floats * root_saved
        both_normed = jnp.concatenate(
            [(floats * norm_rows(floats)).astype(jnp.bfloat16), scaled_saved.astype(jnp.bfloat16)],
            axis=0,
        )
        pre_both = jnp.dot(both_normed, in_full, preferred_element_type=jnp.float32)
        pre_ahead = pre_both[:length].reshape(1, length, groups, 4, HEAD_DIM)
        pre_back = pre_both[length:].reshape(1, length, groups, 4, HEAD_DIM)
        gated_ahead, unused = heads_forward(pre_ahead, keep_ahead, count_ahead)
        partial_sum = jnp.dot(
            gated_ahead.reshape(length, slab_rows), out_full, preferred_element_type=jnp.float32
        )
        summed = lax.psum(partial_sum.astype(jnp.bfloat16), "cores").astype(jnp.float32)
        outgoing = (floats + summed).astype(jnp.bfloat16)
        ahead_out.append(lax.dynamic_slice_in_dim(outgoing, row_start, share, 0))
        if tick_no + 1 < ticks:
            received = from_behind(outgoing, "section", 1)
        gated_back, saved = heads_forward(pre_back, keep_back, count_back)
        grad_gated = (
            jnp.einsum("sd,fd->sf", upstream, out_full, preferred_element_type=jnp.float32)
            .astype(jnp.bfloat16)
            .reshape(1, length, groups, HEAD_DIM)
        )
        grad_pre = heads_backward(pre_back, saved, grad_gated).reshape(length, columns)
        grad_normed = jnp.einsum("sf,df->sd", grad_pre, in_full, preferred_element_type=jnp.float32)
        back_part = root_saved * (
            grad_normed
            - scaled_saved * jnp.mean(grad_normed * scaled_saved, axis=-1, keepdims=True)
        )
        back_sum = lax.psum(back_part.astype(jnp.bfloat16), "cores").astype(jnp.float32)
        grad_in = (upstream.astype(jnp.float32) + back_sum).astype(jnp.bfloat16)
        back_out.append(lax.dynamic_slice_in_dim(grad_in, row_start, share, 0))
        gated_list.append(gated_back.reshape(length, slab_rows))
        upstream_list.append(upstream)
        if tick_no + 1 < ticks:
            returned = from_behind(grad_in, "section", -1)
    stacked_gated = jnp.concatenate(gated_list, axis=0)
    stacked_upstream = jnp.concatenate(upstream_list, axis=0)
    product = lax.dot_general(
        stacked_gated,
        stacked_upstream,
        (((0,), (0,)), ((), ())),
        preferred_element_type=jnp.float32,
    )
    scaling = (ticks * length * lax.axis_size("dp")) ** (-0.5)
    grads_sum = (
        lax.psum_scatter(
            product.astype(jnp.bfloat16), "dp", scatter_dimension=1, tiled=True
        ).astype(jnp.float32)
        * scaling
    )
    return (jnp.stack(ahead_out)[None], jnp.stack(back_out)[None], grads_sum[None])


def solution(mesh):
    in_specs = (
        P(None, "dp", None),
        P("section", "dp", None),
        P(None, "dp", None),
        P("section", "dp", None),
        P("section", None, "dp", None),
        P("section", "dp", "cores"),
        P("section", "cores", "dp"),
        P("dp", None),
        P("dp", None),
        P("dp", None, None, None),
        P("dp", None, None, None),
    )
    out_specs = (
        P("section", None, ("dp", "cores"), None),
        P("section", None, ("dp", "cores"), None),
        P("section", "cores", "dp"),
    )
    return jax.shard_map(
        per_device, mesh=mesh, in_specs=in_specs, out_specs=out_specs, check_vma=False
    )
```

profile of v0, /device:TPU:8, one launch (start us, length us, event | category | flops | bytes accessed | tf_op | source)
XLA Modules:
  0.0 493.3 jit_solution(5450123814144851031)
XLA Ops:
  18.4 73.2 %all-gather.7.cloned.1.call-done = bf16[1,512,2048]{2,1,0:T(8,128)(2,1)} async-done(((bf16[1,512,128]{2,1,0:T(8,128)(2,1)}), bf16[1,512,2048]{2,1,0:T(8,128)(2,1)}) %all-gather.7.cloned.1.call-update) | async-done | bytes 2097168 | tf_op jit(solution)/shard_map/all_gather | solution.py:130
  91.6 2.4 fusion.31
  94.7 104.7 %all-gather.5.cloned.1.call-done = bf16[1,2048,2048]{2,1,0:T(8,128)(2,1)} async-done(((bf16[1,128,2048]{2,1,0:T(8,128)(2,1)}), bf16[1,2048,2048]{2,1,0:T(8,128)(2,1)}) %all-gather.5.cloned.1.call-update) | async-done | bytes 8388624 | tf_op jit(solution)/shard_map/all_gather | solution.py:135
  199.4 5.2 %fusion.6 = f32[192,2048]{1,0:T(8,128)S(1)} fusion(bf16[1,2048,2048]{2,1,0:T(8,128)(2,1)} %all-gather.5.cloned.1.call-done, bf16[96,2048]{1,0:T(8,128)(2,1)S(1)} %get-tuple-element.54, bf16[96,2048]{1,0:T(8,128)(2,1)S(1)} %get-tuple-element.55), kind=kOutput, calls=%fused_computation.6 | convolution fusion | flops 1612185600 | bytes 10747904 | tf_op jit(solution)/shard_map/dot_general | solution.py:165
  216.6 6.5 %fusion.68 = (f32[96]{0:T(128)S(1)}, f32[96]{0:T(128)S(1)}, f32[96,2048]{1,0:T(8,128)S(1)}) fusion(f32[96]{0:T(128)S(1)} %add_rsqrt_fusion.6, bf16[1,2,96,2048]{3,2,1,0:T(8,128)(2,1)S(1)} %copy-done.1, bf16[1,2048,2048]{2,1,0:T(8,128)(2,1)} %all-gather.5.cloned.1.call-done, f32[96,2048]{1,0:T(8,128)} %stack.60, f32[192,2048]{1,0:T(8,128)S(1)} %copy-done.10), kind=kOutput, calls=%fused_computation.86 | convolution fusion | flops 808451840 | bytes 11535616 | tf_op jit(solution)/shard_map/sf,df->sd/dot_general | solution.py:184
  228.6 30.0 %all-reduce.7.cloned.1.call-done = (bf16[96,2048]{1,0:T(8,128)(2,1)}, bf16[96,2048]{1,0:T(8,128)(2,1)}) async-done(((bf16[96,2048]{1,0:T(8,128)(2,1)}, bf16[96,2048]{1,0:T(8,128)(2,1)}), (bf16[96,2048]{1,0:T(8,128)(2,1)}, bf16[96,2048]{1,0:T(8,128)(2,1)})) %all-reduce.7.cloned.1.call-update) | async-done | bytes 786448 | tf_op jit(solution)/shard_map/psum | solution.py:172
  259.8 8.1 %collective-permute-start = (bf16[96,2048]{1,0:T(8,128)(2,1)S(1)}, bf16[96,2048]{1,0:T(8,128)(2,1)S(1)}, u32[]{:S(2)}, u32[]{:S(2)}) collective-permute-start(bf16[96,2048]{1,0:T(8,128)(2,1)S(1)} %fusion.80), channel_id=1, source_target_pairs={{0,32},{32,64},{64,96},{96,128},{128,160},{160,192},{192,224},{224... | collective-permute-start | bytes 1179656 | tf_op jit(solution)/shard_map/ppermute | solution.py:15
  267.9 1.9 add_convert_fusion
  269.8 2.8 collective-permute-start.1
  272.6 26.8 %collective-permute-done = bf16[96,2048]{1,0:T(8,128)(2,1)S(1)} collective-permute-done((bf16[96,2048]{1,0:T(8,128)(2,1)S(1)}, bf16[96,2048]{1,0:T(8,128)(2,1)S(1)}, u32[]{:S(2)}, u32[]{:S(2)}) %collective-permute-start) | collective-permute-done | bytes 393248 | tf_op jit(solution)/shard_map/ppermute | solution.py:15
  299.8 5.2 %fusion.4 = f32[192,2048]{1,0:T(8,128)S(1)} fusion(bf16[1,2048,2048]{2,1,0:T(8,128)(2,1)} %all-gather.5.cloned.1.call-done, bf16[96,2048]{1,0:T(8,128)(2,1)S(1)} %copy-done.21, bf16[96,2048]{1,0:T(8,128)(2,1)S(1)} %multiply_convert_fusion.2), kind=kOutput, calls=%fused_computation.4 | convolution fusion | flops 1612185600 | bytes 10747904 | tf_op jit(solution)/shard_map/dot_general | solution.py:165
  307.5 2.5 reshape.826
  310.0 2.4 fusion.152
  315.3 1.5 fusion.28
  317.8 1.9 multiply_convert_fusion.5
  324.8 2.6 reshape.822
  327.4 2.5 fusion.153
  329.9 2.0 multiply_reduce_fusion.5
  336.3 2.4 stack.67
  338.7 6.8 %fusion.73 = (f32[96]{0:T(128)S(1)}, f32[96,2048]{1,0:T(8,128)S(1)}) fusion(f32[96]{0:T(128)S(1)} %add_rsqrt_fusion.4, bf16[1,2,96,2048]{3,2,1,0:T(8,128)(2,1)} %param.15, bf16[1,2048,2048]{2,1,0:T(8,128)(2,1)} %all-gather.5.cloned.1.call-done, f32[96,2048]{1,0:T(8,128)} %stack.67, f32[192,2048]{1,0:T(8,128)} %copy-done.8), kind=kOutput, calls=%fused_computation.91 | convolution fusion | flops 807862144 | bytes 11141888 | tf_op jit(solution)/shard_map/sf,df->sd/dot_general | solution.py:184
  347.9 1.7 convolution_convert_fusion
  349.7 2.5 copy.74
  354.2 35.7 %all-reduce.5.cloned.1.call-done = (bf16[96,2048]{1,0:T(8,128)(2,1)}, bf16[96,2048]{1,0:T(8,128)(2,1)}) async-done(((bf16[96,2048]{1,0:T(8,128)(2,1)}, bf16[96,2048]{1,0:T(8,128)(2,1)}), (bf16[96,2048]{1,0:T(8,128)(2,1)}, bf16[96,2048]{1,0:T(8,128)(2,1)})) %all-reduce.5.cloned.1.call-update) | async-done | bytes 786448 | tf_op jit(solution)/shard_map/psum | solution.py:172
  393.4 91.7 %reduce-scatter.4.cloned.1.call-done = bf16[128,512]{1,0:T(8,128)(2,1)} async-done(((bf16[2048,512]{1,0:T(8,128)(2,1)}), bf16[128,512]{1,0:T(8,128)(2,1)}) %reduce-scatter.4.cloned.1.call-update) | async-done | bytes 131088
  (156 shorter events, 53.2 us)
Async XLA Ops:
  7.2 11.0 %copy-start.1 = (bf16[1,2,96,2048]{3,2,1,0:T(8,128)(2,1)S(1)}, bf16[1,2,96,2048]{3,2,1,0:T(8,128)(2,1)}, u32[]{:S(2)}) copy-start(bf16[1,2,96,2048]{3,2,1,0:T(8,128)(2,1)} %param.15) | copy-start | bytes 2359300
  7.2 10.9 %copy-start.24 = (bf16[1,96,2048]{2,1,0:T(8,128)(2,1)S(1)}, bf16[1,96,2048]{2,1,0:T(8,128)(2,1)}, u32[]{:S(2)}) copy-start(bf16[1,96,2048]{2,1,0:T(8,128)(2,1)} %param.14) | copy-start | bytes 1179652
  7.2 10.9 %copy-start.17 = (bf16[2,96,2048]{2,1,0:T(8,128)(2,1)S(1)}, bf16[2,96,2048]{2,1,0:T(8,128)(2,1)}, u32[]{:S(2)}) copy-start(bf16[2,96,2048]{2,1,0:T(8,128)(2,1)} %param.13) | copy-start | bytes 2359300
  7.2 84.4 %all-gather.7.cloned.1.call-start = ((), (), s32[]{:S(2)}) async-start(), calls=%async_computation.2 | async-start | bytes 2228224 | tf_op jit(solution)/shard_map/all_gather | solution.py:130
  7.9 191.5 %all-gather.5.cloned.1.call-start = ((), (), s32[]{:S(2)}) async-start(), calls=%async_computation.1 | async-start | bytes 8912896 | tf_op jit(solution)/shard_map/all_gather | solution.py:135
  8.7 249.9 %all-reduce.7.cloned.1.call-start = ((), (), s32[]{:S(2)}) async-start(), calls=%async_computation.5 | async-start | bytes 1572864 | tf_op jit(solution)/shard_map/psum | solution.py:172
  16.0 78.0 %copy-start.5 = (bf16[1,96,2048]{2,1,0:T(8,128)(2,1)}, bf16[1,96,2048]{2,1,0:T(8,128)(2,1)S(1)}, u32[]{:S(2)}) copy-start(bf16[1,96,2048]{2,1,0:T(8,128)(2,1)S(1)} %get-tuple-element.28) | copy-start | bytes 1179652
  224.3 34.3 %copy-start.6 = (bf16[1,96,2048]{2,1,0:T(8,128)(2,1)S(1)}, bf16[1,96,2048]{2,1,0:T(8,128)(2,1)}, u32[]{:S(2)}) copy-start(bf16[1,96,2048]{2,1,0:T(8,128)(2,1)} %copy-done.5) | copy-start | bytes 1179652
  226.3 163.6 %all-reduce.5.cloned.1.call-start = ((), (), s32[]{:S(2)}) async-start(), calls=%async_computation.4 | async-start | bytes 1572864 | tf_op jit(solution)/shard_map/psum | solution.py:172
  228.6 84.0 %copy-start.27 = (f32[96,96]{1,0:T(8,128)}, f32[96,96]{1,0:T(8,128)S(1)}, u32[]{:S(2)}) copy-start(f32[96,96]{1,0:T(8,128)S(1)} %fusion.53) | copy-start | bytes 110596
  258.6 40.8 %copy-start.16 = (bf16[2,96,2048]{2,1,0:T(8,128)(2,1)S(1)}, bf16[2,96,2048]{2,1,0:T(8,128)(2,1)}, u32[]{:S(2)}) copy-start(bf16[2,96,2048]{2,1,0:T(8,128)(2,1)} %param.11) | copy-start | bytes 2359300
  259.8 12.8 %copy-start.13 = (bf16[96,2048]{1,0:T(8,128)(2,1)}, bf16[96,2048]{1,0:T(8,128)(2,1)S(1)}, u32[]{:S(2)}) copy-start(bf16[96,2048]{1,0:T(8,128)(2,1)S(1)} %fusion.80) | copy-start | bytes 1179652
  259.8 40.0 %copy-start.21 = (bf16[96,2048]{1,0:T(8,128)(2,1)S(1)}, bf16[96,2048]{1,0:T(8,128)(2,1)}, u32[]{:S(2)}) copy-start(bf16[96,2048]{1,0:T(8,128)(2,1)} %get-tuple-element.37) | copy-start | bytes 1179652
  259.8 39.6 %collective-permute-start = (bf16[96,2048]{1,0:T(8,128)(2,1)S(1)}, bf16[96,2048]{1,0:T(8,128)(2,1)S(1)}, u32[]{:S(2)}, u32[]{:S(2)}) collective-permute-start(bf16[96,2048]{1,0:T(8,128)(2,1)S(1)} %fusion.80), channel_id=1, source_target_pairs={{0,32},{32,64},{64,96},{96,128},{128,160},{160,192},{192,224},{224... | collective-permute-start | bytes 1179656 | tf_op jit(solution)/shard_map/ppermute | solution.py:15
  269.8 43.7 %collective-permute-start.1 = (bf16[96,2048]{1,0:T(8,128)(2,1)}, bf16[96,2048]{1,0:T(8,128)(2,1)}, u32[]{:S(2)}, u32[]{:S(2)}) collective-permute-start(bf16[96,2048]{1,0:T(8,128)(2,1)} %add_convert_fusion), channel_id=1, source_target_pairs={{32,0},{64,32},{96,64},{128,96},{160,128},{192,160},{224,192},{256... | collective-permute-start | bytes 1179656 | tf_op jit(solution)/shard_map/ppermute | solution.py:15
  310.0 3.5 copy-start.18
  317.8 4.4 copy-start.12
  317.8 6.1 %copy-start.26 = (f32[4,96,96]{2,1,0:T(8,128)S(1)}, f32[4,96,96]{2,1,0:T(8,128)}, u32[]{:S(2)}) copy-start(f32[4,96,96]{2,1,0:T(8,128)} %copy-done.25) | copy-start | bytes 442372
  317.8 6.1 %copy-start.28 = (f32[96,96]{1,0:T(8,128)S(1)}, f32[96,96]{1,0:T(8,128)}, u32[]{:S(2)}) copy-start(f32[96,96]{1,0:T(8,128)} %copy-done.27) | copy-start | bytes 110596
  327.4 6.3 %copy-start.15 = (f32[1,96,4,1,128]{4,1,2,3,0:T(8,128)S(1)}, f32[1,96,4,1,128]{4,1,2,3,0:T(8,128)}, u32[]{:S(2)}) copy-start(f32[1,96,4,1,128]{4,1,2,3,0:T(8,128)} %get-tuple-element.39) | copy-start | bytes 589828
  338.7 6.8 %copy-start.2 = (bf16[1,2,96,2048]{3,2,1,0:T(8,128)(2,1)S(1)}, bf16[1,2,96,2048]{3,2,1,0:T(8,128)(2,1)}, u32[]{:S(2)}) copy-start(bf16[1,2,96,2048]{3,2,1,0:T(8,128)(2,1)} %param.15) | copy-start | bytes 2359300
  338.7 7.8 %copy-start.20 = (bf16[1,96,4,128]{3,2,1,0:T(4,128)(2,1)S(1)}, bf16[1,96,4,128]{3,2,1,0:T(4,128)(2,1)}, u32[]{:S(2)}) copy-start(bf16[1,96,4,128]{3,2,1,0:T(4,128)(2,1)} %copy.53) | copy-start | bytes 294916
  347.7 137.4 %reduce-scatter.4.cloned.1.call-start = ((), (), s32[]{:S(2)}) async-start(), calls=%async_computation.3 | async-start | bytes 2228224
  352.2 38.6 %copy-start.4 = (bf16[96,2048]{1,0:T(8,128)(2,1)S(1)}, bf16[96,2048]{1,0:T(8,128)(2,1)}, u32[]{:S(2)}) copy-start(bf16[96,2048]{1,0:T(8,128)(2,1)} %copy-done.3) | copy-start | bytes 1179652
  (14 other events, 20.4 us)
Sparse Core Ops, SparseCore 0:
  10.0 81.4 all-gather.6
  93.7 105.7 all-gather.4
  226.4 32.1 all-reduce.6
  347.8 42.0 all-reduce.4
  392.6 92.4 reduce-scatter.3
where the time goes:
time: 494 us; the launch traced here: 493 us
  waiting for transfers between devices  364 us (74%)
  matrix products  45.3 us (9%)
  other arithmetic  30.4 us (6%)
  local copies, waits for them, and re-layouts  25.8 us (5%)
  between operations  17.2 us (3%)
  starting transfers between devices  11.1 us (2%)
    all_gather x1, waiting for transfers between devices, per_device(): in_full = lax.all_gather(in_weight[0], 'dp', axis=0, tiled=True)  105 us
    unnamed x6, waiting for transfers between devices  93.1 us
    all_gather x1, waiting for transfers between devices, per_device(): out_full = lax.all_gather(out_weight[0], 'dp', axis=1, tiled=True)  73.2 us
    psum x2, waiting for transfers between devices, per_device(): lax.psum(partial_sum.astype(jnp.bfloat16), 'cores').astype(jnp.float32)  65.7 us
    ppermute x2, waiting for transfers between devices, from_behind(): return lax.ppermute(x, axis, pairs)  26.8 us
    dot_general x2, matrix products, per_device(): jnp.einsum('sf,df->sd', grad_pre, in_full, preferred_element_type=jnp.flo...  13.3 us
    ppermute x2, starting transfers between devices, from_behind(): return lax.ppermute(x, axis, pairs)  10.9 us
    dot_general x2, matrix products, per_device(): pre_both = jnp.dot(both_normed, in_full, preferred_element_type=jnp.float32)  10.4 us
  transfers between devices with their start and end apart: 7, of which 6 were waited for; matrix products, arithmetic and copies ran while one was open for 7% of the time, Pallas kernels for 0%

commit v1 on v0

--- a/solution.py
+++ b/solution.py
@@ -169,7 +169,9 @@
         partial_sum = jnp.dot(
             gated_ahead.reshape(length, slab_rows), out_full, preferred_element_type=jnp.float32
         )
-        summed = lax.psum(partial_sum.astype(jnp.bfloat16), "cores").astype(jnp.float32)
+        summed = jnp.sum(lax.all_gather(partial_sum.astype(jnp.bfloat16), "cores"), axis=0).astype(
+            jnp.float32
+        )
         outgoing = (floats + summed).astype(jnp.bfloat16)
         ahead_out.append(lax.dynamic_slice_in_dim(outgoing, row_start, share, 0))
         if tick_no + 1 < ticks:

time: 494 us -> 466 us (0.943)
  the two profiles are of different devices: /device:TPU:8 before, /device:TPU:24 now
where the time goes in v1:
time: 466 us; the launch traced here: 465 us
  waiting for transfers between devices  320 us (69%)
  matrix products  46 us (10%)
  other arithmetic  35.1 us (8%)
  local copies, waits for them, and re-layouts  27.7 us (6%)
  between operations  17.2 us (4%)
  starting transfers between devices  13.7 us (3%)
  blocking collectives  5 us (1%)
    all_gather x1, waiting for transfers between devices, per_device(): in_full = lax.all_gather(in_weight[0], 'dp', axis=0, tiled=True)  105 us
    unnamed x6, waiting for transfers between devices  95.1 us
    all_gather x1, waiting for transfers between devices, per_device(): out_full = lax.all_gather(out_weight[0], 'dp', axis=1, tiled=True)  71.2 us
    psum x2, waiting for transfers between devices, per_device(): lax.psum(back_part.astype(jnp.bfloat16), 'cores').astype(jnp.float32)  27.2 us
    ppermute x2, waiting for transfers between devices, from_behind(): return lax.ppermute(x, axis, pairs)  21 us
    dot_general x2, matrix products, per_device(): jnp.einsum('sf,df->sd', grad_pre, in_full, preferred_element_type=jnp.flo...  13.5 us
    ppermute x2, starting transfers between devices, from_behind(): return lax.ppermute(x, axis, pairs)  13.3 us
    dot_general x2, matrix products, per_device(): pre_both = jnp.dot(both_normed, in_full, preferred_element_type=jnp.float32)  10.5 us
  transfers between devices with their start and end apart: 7, of which 7 were waited for; matrix products, arithmetic and copies ran while one was open for 13% of the time, Pallas kernels for 0%

profile of v1, /device:TPU:24, one launch (start us, length us, event | category | flops | bytes accessed | tf_op | source)
XLA Modules:
  0.0 464.5 jit_solution(10608705359505877777)
XLA Ops:
  20.2 71.2 %all-gather.9.cloned.1.call-done = bf16[1,512,2048]{2,1,0:T(8,128)(2,1)} async-done(((bf16[1,512,128]{2,1,0:T(8,128)(2,1)}), bf16[1,512,2048]{2,1,0:T(8,128)(2,1)}) %all-gather.9.cloned.1.call-update) | async-done | bytes 2097168 | tf_op jit(solution)/shard_map/all_gather | solution.py:130
  91.4 2.4 fusion.31
  93.8 105.4 %all-gather.7.cloned.1.call-done = bf16[1,2048,2048]{2,1,0:T(8,128)(2,1)} async-done(((bf16[1,128,2048]{2,1,0:T(8,128)(2,1)}), bf16[1,2048,2048]{2,1,0:T(8,128)(2,1)}) %all-gather.7.cloned.1.call-update) | async-done | bytes 8388624 | tf_op jit(solution)/shard_map/all_gather | solution.py:135
  199.2 5.2 %fusion.6 = f32[192,2048]{1,0:T(8,128)S(1)} fusion(bf16[1,2048,2048]{2,1,0:T(8,128)(2,1)} %all-gather.7.cloned.1.call-done, bf16[96,2048]{1,0:T(8,128)(2,1)S(1)} %get-tuple-element.48, bf16[96,2048]{1,0:T(8,128)(2,1)S(1)} %get-tuple-element.49), kind=kOutput, calls=%fused_computation.6 | convolution fusion | flops 1612185600 | bytes 10747904 | tf_op jit(solution)/shard_map/dot_general | solution.py:165
  214.4 2.6 fusion.156
  220.7 2.5 all-gather.2
  227.3 5.3 %collective-permute-start = (bf16[96,2048]{1,0:T(8,128)(2,1)}, bf16[96,2048]{1,0:T(8,128)(2,1)}, u32[]{:S(2)}, u32[]{:S(2)}) collective-permute-start(bf16[96,2048]{1,0:T(8,128)(2,1)} %fusion.80), channel_id=1, source_target_pairs={{0,32},{32,64},{64,96},{96,128},{128,160},{160,192},{192,224},{224... | collective-permute-start | bytes 1179656 | tf_op jit(solution)/shard_map/ppermute | solution.py:15
  235.2 2.4 stack.60
  237.6 6.8 %fusion.68 = (f32[96]{0:T(128)S(1)}, f32[96]{0:T(128)S(1)}, f32[96,2048]{1,0:T(8,128)S(1)}) fusion(f32[96]{0:T(128)S(1)} %add_rsqrt_fusion.6, bf16[1,2,96,2048]{3,2,1,0:T(8,128)(2,1)S(1)} %copy-done.1, bf16[1,2048,2048]{2,1,0:T(8,128)(2,1)} %all-gather.7.cloned.1.call-done, f32[96,2048]{1,0:T(8,128)} %stack.60, f32[192,2048]{1,0:T(8,128)} %copy-done.6), kind=kOutput, calls=%fused_computation.86 | convolution fusion | flops 808451840 | bytes 11535488 | tf_op jit(solution)/shard_map/sf,df->sd/dot_general | solution.py:186
  245.9 8.0 %collective-permute-done = bf16[96,2048]{1,0:T(8,128)(2,1)} collective-permute-done((bf16[96,2048]{1,0:T(8,128)(2,1)}, bf16[96,2048]{1,0:T(8,128)(2,1)}, u32[]{:S(2)}, u32[]{:S(2)}) %collective-permute-start) | collective-permute-done | bytes 393248 | tf_op jit(solution)/shard_map/ppermute | solution.py:15
  255.3 5.3 %fusion.4 = f32[192,2048]{1,0:T(8,128)S(1)} fusion(bf16[1,2048,2048]{2,1,0:T(8,128)(2,1)} %all-gather.7.cloned.1.call-done, bf16[96,2048]{1,0:T(8,128)(2,1)S(1)} %copy-done.13, bf16[96,2048]{1,0:T(8,128)(2,1)S(1)} %multiply_convert_fusion.2), kind=kOutput, calls=%fused_computation.4 | convolution fusion | flops 1612185600 | bytes 10747904 | tf_op jit(solution)/shard_map/dot_general | solution.py:165
  263.1 2.5 reshape.826
  265.7 2.5 fusion.152
  268.2 8.4 %all-reduce.3.cloned.1.call-done = bf16[96,2048]{1,0:T(8,128)(2,1)} async-done(((bf16[96,2048]{1,0:T(8,128)(2,1)}), bf16[96,2048]{1,0:T(8,128)(2,1)}) %all-reduce.3.cloned.1.call-update) | async-done | bytes 393232 | tf_op jit(solution)/shard_map/psum | solution.py:191
  277.8 8.0 %collective-permute-start.1 = (bf16[96,2048]{1,0:T(8,128)(2,1)S(1)}, bf16[96,2048]{1,0:T(8,128)(2,1)S(1)}, u32[]{:S(2)}, u32[]{:S(2)}) collective-permute-start(bf16[96,2048]{1,0:T(8,128)(2,1)S(1)} %add_convert_fusion), channel_id=1, source_target_pairs={{32,0},{64,32},{96,64},{128,96},{160,128},{192,160},{224,192},{256... | collective-permute-start | bytes 1179656 | tf_op jit(solution)/shard_map/ppermute | solution.py:15
  288.7 13.0 %collective-permute-done.1 = bf16[96,2048]{1,0:T(8,128)(2,1)S(1)} collective-permute-done((bf16[96,2048]{1,0:T(8,128)(2,1)S(1)}, bf16[96,2048]{1,0:T(8,128)(2,1)S(1)}, u32[]{:S(2)}, u32[]{:S(2)}) %collective-permute-start.1) | collective-permute-done | bytes 393248 | tf_op jit(solution)/shard_map/ppermute | solution.py:15
  311.4 2.3 stack.67
  313.7 6.8 %fusion.73 = (f32[96]{0:T(128)S(1)}, f32[96,2048]{1,0:T(8,128)S(1)}) fusion(f32[96]{0:T(128)S(1)} %add_rsqrt_fusion.4, bf16[1,2,96,2048]{3,2,1,0:T(8,128)(2,1)} %param.15, bf16[1,2048,2048]{2,1,0:T(8,128)(2,1)} %all-gather.7.cloned.1.call-done, f32[96,2048]{1,0:T(8,128)} %stack.67, f32[192,2048]{1,0:T(8,128)} %copy-done.7), kind=kOutput, calls=%fused_computation.91 | convolution fusion | flops 807862144 | bytes 11141888 | tf_op jit(solution)/shard_map/sf,df->sd/dot_general | solution.py:186
  321.8 3.0 convolution_convert_fusion
  324.8 3.9 copy.74
  330.8 2.6 reshape.822
  338.5 2.5 all-gather.3
  342.0 18.8 %all-reduce.5.cloned.1.call-done = bf16[96,2048]{1,0:T(8,128)(2,1)} async-done(((bf16[96,2048]{1,0:T(8,128)(2,1)}), bf16[96,2048]{1,0:T(8,128)(2,1)}) %all-reduce.5.cloned.1.call-update) | async-done | bytes 393232 | tf_op jit(solution)/shard_map/psum | solution.py:191
  362.6 93.6 %reduce-scatter.4.cloned.1.call-done = bf16[128,512]{1,0:T(8,128)(2,1)} async-done(((bf16[2048,512]{1,0:T(8,128)(2,1)}), bf16[128,512]{1,0:T(8,128)(2,1)}) %reduce-scatter.4.cloned.1.call-update) | async-done | bytes 131088
  (141 shorter events, 62.3 us)
Async XLA Ops:
  7.2 12.8 %copy-start.1 = (bf16[1,2,96,2048]{3,2,1,0:T(8,128)(2,1)S(1)}, bf16[1,2,96,2048]{3,2,1,0:T(8,128)(2,1)}, u32[]{:S(2)}) copy-start(bf16[1,2,96,2048]{3,2,1,0:T(8,128)(2,1)} %param.15) | copy-start | bytes 2359300
  7.2 12.7 %copy-start.16 = (bf16[1,96,2048]{2,1,0:T(8,128)(2,1)S(1)}, bf16[1,96,2048]{2,1,0:T(8,128)(2,1)}, u32[]{:S(2)}) copy-start(bf16[1,96,2048]{2,1,0:T(8,128)(2,1)} %param.14) | copy-start | bytes 1179652
  7.2 12.7 %copy-start.11 = (bf16[2,96,2048]{2,1,0:T(8,128)(2,1)S(1)}, bf16[2,96,2048]{2,1,0:T(8,128)(2,1)}, u32[]{:S(2)}) copy-start(bf16[2,96,2048]{2,1,0:T(8,128)(2,1)} %param.13) | copy-start | bytes 2359300
  7.2 84.2 %all-gather.9.cloned.1.call-start = ((), (), s32[]{:S(2)}) async-start(), calls=%async_computation.4 | async-start | bytes 2228224 | tf_op jit(solution)/shard_map/all_gather | solution.py:130
  7.9 191.3 %all-gather.7.cloned.1.call-start = ((), (), s32[]{:S(2)}) async-start(), calls=%async_computation.3 | async-start | bytes 8912896 | tf_op jit(solution)/shard_map/all_gather | solution.py:135
  8.7 267.9 %all-reduce.3.cloned.1.call-start = ((), (), s32[]{:S(2)}) async-start(), calls=%async_computation.1 | async-start | bytes 786432 | tf_op jit(solution)/shard_map/psum | solution.py:191
  17.9 75.8 %copy-start.5 = (bf16[1,96,2048]{2,1,0:T(8,128)(2,1)}, bf16[1,96,2048]{2,1,0:T(8,128)(2,1)S(1)}, u32[]{:S(2)}) copy-start(bf16[1,96,2048]{2,1,0:T(8,128)(2,1)S(1)} %get-tuple-element.24) | copy-start | bytes 1179652
  19.4 188.6 %copy-start.19 = (f32[96,96]{1,0:T(8,128)}, f32[96,96]{1,0:T(8,128)S(1)}, u32[]{:S(2)}) copy-start(f32[96,96]{1,0:T(8,128)S(1)} %fusion.48) | copy-start | bytes 110596
  208.3 3.7 copy-start.20
  214.4 5.8 %copy-start = (bf16[1,512,2048]{2,1,0:T(8,128)(2,1)S(1)}, bf16[1,512,2048]{2,1,0:T(8,128)(2,1)}, u32[]{:S(2)}) copy-start(bf16[1,512,2048]{2,1,0:T(8,128)(2,1)} %all-gather.9.cloned.1.call-done) | copy-start | bytes 6291460
  227.3 26.5 %collective-permute-start = (bf16[96,2048]{1,0:T(8,128)(2,1)}, bf16[96,2048]{1,0:T(8,128)(2,1)}, u32[]{:S(2)}, u32[]{:S(2)}) collective-permute-start(bf16[96,2048]{1,0:T(8,128)(2,1)} %fusion.80), channel_id=1, source_target_pairs={{0,32},{32,64},{64,96},{96,128},{128,160},{160,192},{192,224},{224... | collective-permute-start | bytes 1179656 | tf_op jit(solution)/shard_map/ppermute | solution.py:15
  245.6 115.2 %all-reduce.5.cloned.1.call-start = ((), (), s32[]{:S(2)}) async-start(), calls=%async_computation.2 | async-start | bytes 786432 | tf_op jit(solution)/shard_map/psum | solution.py:191
  245.8 9.5 %copy-start.13 = (bf16[96,2048]{1,0:T(8,128)(2,1)S(1)}, bf16[96,2048]{1,0:T(8,128)(2,1)}, u32[]{:S(2)}) copy-start(bf16[96,2048]{1,0:T(8,128)(2,1)} %get-tuple-element.34) | copy-start | bytes 1179652
  276.6 25.2 %copy-start.12 = (bf16[2,96,2048]{2,1,0:T(8,128)(2,1)S(1)}, bf16[2,96,2048]{2,1,0:T(8,128)(2,1)}, u32[]{:S(2)}) copy-start(bf16[2,96,2048]{2,1,0:T(8,128)(2,1)} %param.13) | copy-start | bytes 2359300
  277.8 11.0 %copy-start.9 = (bf16[96,2048]{1,0:T(8,128)(2,1)}, bf16[96,2048]{1,0:T(8,128)(2,1)S(1)}, u32[]{:S(2)}) copy-start(bf16[96,2048]{1,0:T(8,128)(2,1)S(1)} %add_convert_fusion) | copy-start | bytes 1179652
  277.8 24.0 %collective-permute-start.1 = (bf16[96,2048]{1,0:T(8,128)(2,1)S(1)}, bf16[96,2048]{1,0:T(8,128)(2,1)S(1)}, u32[]{:S(2)}, u32[]{:S(2)}) collective-permute-start(bf16[96,2048]{1,0:T(8,128)(2,1)S(1)} %add_convert_fusion), channel_id=1, source_target_pairs={{32,0},{64,32},{96,64},{128,96},{160,128},{192,160},{224,192},{256... | collective-permute-start | bytes 1179656 | tf_op jit(solution)/shard_map/ppermute | solution.py:15
  286.9 1.9 copy-start.17
  305.0 4.2 copy-start.8
  305.0 4.6 copy-start.18
  313.7 6.8 %copy-start.2 = (bf16[1,2,96,2048]{3,2,1,0:T(8,128)(2,1)S(1)}, bf16[1,2,96,2048]{3,2,1,0:T(8,128)(2,1)}, u32[]{:S(2)}) copy-start(bf16[1,2,96,2048]{3,2,1,0:T(8,128)(2,1)} %param.15) | copy-start | bytes 2359300
  313.7 7.9 %copy-start.14 = (bf16[1,96,4,128]{3,1,2,0:T(8,128)(2,1)S(1)}, bf16[1,96,4,128]{3,1,2,0:T(8,128)(2,1)}, u32[]{:S(2)}) copy-start(bf16[1,96,4,128]{3,1,2,0:T(8,128)(2,1)} %get-tuple-element.29) | copy-start | bytes 294916
  321.5 134.7 %reduce-scatter.4.cloned.1.call-start = ((), (), s32[]{:S(2)}) async-start(), calls=%async_computation.5 | async-start | bytes 2228224
  338.4 2.7 copy-start.10
  338.5 22.4 %copy-start.4 = (bf16[96,2048]{1,0:T(8,128)(2,1)S(1)}, bf16[96,2048]{1,0:T(8,128)(2,1)}, u32[]{:S(2)}) copy-start(bf16[96,2048]{1,0:T(8,128)(2,1)} %copy-done.3) | copy-start | bytes 1179652
  (4 other events, 4.6 us)
Sparse Core Ops, SparseCore 0:
  10.0 81.2 all-gather.8
  93.5 105.7 all-gather.6
  245.7 30.7 all-reduce.2
  321.6 39.1 all-reduce.4
  363.5 92.6 reduce-scatter.3
